TPU v7x, 32 devices: a whole 2x2x4 slice. The times are simulated.
32 devices in a mesh: dp: 8 (over z, y), tensor: 4 (over x, core).
Axes of the slice: x: 2, y: 2, z: 4, core: 2. Of those that a mesh axis runs over, the one named last changes fastest.
Arguments:
- input_token_ids: int32 [4, 32, 512], P(None, ('dp', 'tensor')), may hold values from 0 to 50264
- segments: int32 [4, 32, 512], P(None, ('dp', 'tensor')), may hold values from -1 to 63, as said below
- labels: float32 [4, 32, 64], P(None, ('dp', 'tensor')), may hold values from 0 to 5
- embedding: bfloat16 [768, 50265], P('tensor'), may hold values from -6 to 6
- position_embedding_table: bfloat16 [512, 768], replicated, may hold values from -3 to 3
- norm_gain_rows: float32 [3, 768], replicated, may hold values from 0.5 to 1.5
- norm_shift_rows: float32 [3, 768], replicated, may hold values from -0.3 to 0.3
- query_key_value_weight: bfloat16 [3, 768, 768], replicated, may hold values from -0.21875 to 0.21875
- attention_output_weight: bfloat16 [768, 768], replicated, may hold values from -0.625 to 0.625
- attention_bias_stack: float32 [5, 768], replicated, may hold values from -0.3 to 0.3
- feedforward_in_weight: bfloat16 [768, 3072], P(None, 'tensor'), may hold values from -0.21875 to 0.21875
- feedforward_bias: bfloat16 [3072], P('tensor'), may hold values from -0.59765625 to 0.59765625
- feedforward_out_weight: bfloat16 [3072, 768], P('tensor'), may hold values from -0.109375 to 0.109375
- adapter_down_weight: bfloat16 [2, 768, 8], replicated, may hold values from -0.21875 to 0.21875
- adapter_up_weight: float32 [2, 8, 768], replicated, may hold values from -0.3 to 0.3
- adapter_momentum: float32 [2, 8, 768], replicated, may hold values from -0.0017089844 to 0.0017089844
- head: float32 [769], replicated, may hold values from -0.21875 to 0.21875
- head_first_moment: float32 [769], replicated, may hold values from -0.015625 to 0.015625
- head_second_moment: float32 [769], replicated, may hold values from 6e-08 to 2.6e-07
Outputs:
- squared_error_sum: float32 [], replicated
- item_count: float32 [], replicated
- global_gradient_norm: float32 [], replicated
- adapter_moment_next: float32 [2, 8, 768], replicated
- adapter_up_updated: float32 [2, 8, 768], replicated
- lora_low: bfloat16 [2, 8, 768], replicated
- head_moment_next: float32 [769], replicated
- head_square_next: float32 [769], replicated
- head_updated: float32 [769], replicated
- head_low: bfloat16 [769], replicated
Inputs may be any that keep to these rules, and one draw needn't show every extreme that they name: `segments`: each sequence holds whole items from its first row on, numbered 0, 1, 2, ... in order, each of 8 to 128 rows; the rows after the last item are -1. In the first micro-batch one sequence is filled entirely with items of 8 rows, so item numbers reach 63.
All inputs are finite; a program needn't handle non-finite values.
Results may differ from a plain program's by a relative error of at most 0.0055.
Values may be sent and summed in bfloat16 or wider, within the bound.
No kernel may reach another device: no remote copies, remote signals or barrier semaphores. Data moves between devices by JAX's collectives and lax.ppermute only.
A program may use at most 320 MiB of HBM per device.

v0:
```python
import jax
import jax.numpy as jnp
from jax import lax
from jax.sharding import PartitionSpec as P

MODEL_WIDTH = 768
HEADS = 12
HEAD_DIM = 64
STEP = 10


LN_EPS = 1e-05
CLIP_NORM = 0.5
ADAPTER_SCALE = 2.0
ORTHO_MOMENTUM = 0.5
ORTHO_STEP_SIZE = 1.0
NS_A = 3.4445
NS_B = -4.775
NS_C = 2.0315
BETA_ONE = 0.9
BETA_TWO = 0.999
ADAM_RATE = 0.05
ADAM_EPS = 1e-08
DECAY = 0.01
TOP_PRECISION = lax.Precision.HIGHEST
CONTRACT = (((1,), (1,)), ((), ()))


def layer_norm(value_rows, gain_row, shift_row):
    center = jnp.mean(value_rows, -1, keepdims=True)
    offset = value_rows - center
    spread = jnp.mean(offset * offset, -1, keepdims=True)
    return offset * lax.rsqrt(spread + LN_EPS) * gain_row + shift_row


def norm_back(value_rows, gain_row, shift_row, grad_out):
    return jax.vjp(lambda inner: layer_norm(inner, gain_row, shift_row), value_rows)[1](grad_out)[0]


def within_item(segment):
    sequence_length = segment.shape[-1]
    column = jnp.arange(sequence_length, dtype=jnp.int32)
    before = jnp.concatenate(
        [jnp.full(segment.shape[:-1] + (1,), -2, jnp.int32), segment[..., :-1]], -1
    )
    opening = jnp.where(segment != before, column, 0)
    return column - lax.cummax(opening, axis=segment.ndim - 1)


def exact_gelu(value_rows):
    return jax.nn.gelu(value_rows, approximate=False)


def attention_probs(query_r, key_r, segment):
    scores = jnp.einsum("sqhd,skhd->shqk", query_r, key_r, preferred_element_type=jnp.float32)
    allowed = (segment[:, :, None] == segment[:, None, :])[:, None]
    return jax.nn.softmax(jnp.where(allowed, scores * HEAD_DIM ** (-0.5), -1000000000.0), axis=-1)


def ffn_forward(normed1_r, weight_list):
    input_weight, input_bias, output_weight = weight_list
    bias_in = input_bias.astype(jnp.float32)
    pre_act = (
        jnp.dot(
            lax.all_gather(normed1_r, "tensor", axis=0, tiled=True),
            input_weight,
            preferred_element_type=jnp.float32,
        )
        + bias_in
    )
    act_r = exact_gelu(pre_act).astype(jnp.bfloat16)
    result = lax.psum_scatter(
        jnp.dot(act_r, output_weight, preferred_element_type=jnp.float32),
        "tensor",
        scatter_dimension=0,
        tiled=True,
    )
    return (pre_act, result)


def ffn_backward(grad_r, pre_act, weight_list):
    input_weight, input_bias, output_weight = weight_list
    back_act = lax.dot_general(
        lax.all_gather(grad_r, "tensor", axis=0, tiled=True),
        output_weight,
        CONTRACT,
        preferred_element_type=jnp.float32,
    )
    grad_pre = jax.vjp(exact_gelu, pre_act)[1](back_act)[0].astype(jnp.bfloat16)
    return lax.psum_scatter(
        lax.dot_general(grad_pre, input_weight, CONTRACT, preferred_element_type=jnp.float32),
        "tensor",
        scatter_dimension=0,
        tiled=True,
    )


def forward_layer(ids_block, segment, label, parameter_tree, weight_list):
    (
        embedding,
        position_embedding_table,
        norm_gain_rows,
        norm_shift_rows,
        query_key_value_weight,
        attention_output_weight,
        attention_bias_stack,
        adapter_down_weight,
        adapter_lowered_up,
        head,
    ) = parameter_tree
    sequence_count, sequence_length = ids_block.shape
    shape_four = (sequence_count, sequence_length, HEADS, HEAD_DIM)
    all_ids = lax.all_gather(ids_block, "tensor", axis=0, tiled=True)
    picked = jnp.take(embedding, all_ids.reshape(-1), axis=1)
    token_cols = lax.all_to_all(picked, "tensor", split_axis=1, concat_axis=0, tiled=True)
    position = within_item(segment).reshape(-1)
    start_rows = token_cols.T.astype(jnp.float32) + jnp.take(
        position_embedding_table, position, axis=0
    ).astype(jnp.float32)
    normed0 = layer_norm(start_rows, norm_gain_rows[0], norm_shift_rows[0])
    lowered_input0 = normed0.astype(jnp.bfloat16)
    apply_projection = jnp.einsum(
        "rd,kde->kre", lowered_input0, query_key_value_weight, preferred_element_type=jnp.float32
    )
    reduced_gradients = jnp.einsum(
        "zl,oly->ozy", lowered_input0, adapter_down_weight, preferred_element_type=jnp.float32
    ).astype(jnp.bfloat16)
    adapted_weight = jnp.einsum(
        "qip,qpt->qit", reduced_gradients, adapter_lowered_up, preferred_element_type=jnp.float32
    )
    query_r = (
        (apply_projection[0] + attention_bias_stack[0] + ADAPTER_SCALE * adapted_weight[0])
        .astype(jnp.bfloat16)
        .reshape(shape_four)
    )
    key_r = (apply_projection[1] + attention_bias_stack[1]).astype(jnp.bfloat16).reshape(shape_four)
    value_r = (
        (apply_projection[2] + attention_bias_stack[2] + ADAPTER_SCALE * adapted_weight[1])
        .astype(jnp.bfloat16)
        .reshape(shape_four)
    )
    attn_probs = attention_probs(query_r, key_r, segment)
    mixed_r = (
        jnp.einsum(
            "shqk,skhd->sqhd",
            attn_probs.astype(jnp.bfloat16),
            value_r,
            preferred_element_type=jnp.float32,
        )
        .reshape(-1, MODEL_WIDTH)
        .astype(jnp.bfloat16)
    )
    resid1 = normed0 + (
        jnp.dot(mixed_r, attention_output_weight, preferred_element_type=jnp.float32)
        + attention_bias_stack[3]
    )
    normed1 = layer_norm(resid1, norm_gain_rows[1], norm_shift_rows[1])
    pre_act, ffn_part = ffn_forward(normed1.astype(jnp.bfloat16), weight_list)
    resid2 = normed1 + (ffn_part + attention_bias_stack[4])
    normalized_second = layer_norm(resid2, norm_gain_rows[2], norm_shift_rows[2])
    slots = jnp.arange(label.shape[-1], dtype=jnp.int32)
    batch_member = (segment[:, None, :] == slots[None, :, None]).astype(jnp.float32)
    counts = jnp.sum(batch_member, -1)
    pooled = (
        jnp.einsum(
            "hro,hon->hrn",
            batch_member,
            normalized_second.reshape(sequence_count, sequence_length, -1),
            precision=TOP_PRECISION,
        )
        / jnp.maximum(counts, 1.0)[..., None]
    )
    predicted = jnp.einsum("sid,d->si", pooled, head[:-1], precision=TOP_PRECISION) + head[-1]
    pred_error = jnp.where(counts > 0, predicted - label, 0.0)
    saved_activations = (
        segment,
        reduced_gradients,
        query_r,
        key_r,
        value_r,
        resid1,
        resid2,
        pre_act,
        batch_member,
        counts,
        pooled,
        pred_error,
    )
    return (jnp.sum(pred_error * pred_error), saved_activations)


def layer_backward_pass(saved_activations, parameter_tree, weight_list, item_gradient_sum):
    (
        embedding,
        position_embedding_table,
        norm_gain_rows,
        norm_shift_rows,
        query_key_value_weight,
        attention_output_weight,
        attention_bias_stack,
        adapter_down_weight,
        adapter_lowered_up,
        head,
    ) = parameter_tree
    (
        segment,
        reduced_gradients,
        query_r,
        key_r,
        value_r,
        resid1,
        resid2,
        pre_act,
        batch_member,
        counts,
        pooled,
        pred_error,
    ) = saved_activations
    grad_pred = 2.0 * pred_error / item_gradient_sum
    head_gradient = jnp.concatenate(
        [
            jnp.einsum("si,sid->d", grad_pred, pooled, precision=TOP_PRECISION),
            jnp.sum(grad_pred)[None],
        ]
    )
    pooled_gradient = grad_pred[..., None] * head[:-1] / jnp.maximum(counts, 1.0)[..., None]
    gradient_normalized2 = jnp.einsum(
        "bht,bhr->btr", batch_member, pooled_gradient, precision=TOP_PRECISION
    ).reshape(-1, MODEL_WIDTH)
    grad_resid2 = norm_back(resid2, norm_gain_rows[2], norm_shift_rows[2], gradient_normalized2)
    grad_normed1 = grad_resid2 + ffn_backward(
        grad_resid2.astype(jnp.bfloat16), pre_act, weight_list
    )
    grad_resid1 = norm_back(resid1, norm_gain_rows[1], norm_shift_rows[1], grad_normed1)
    grad_mixed = lax.dot_general(
        grad_resid1.astype(jnp.bfloat16),
        attention_output_weight,
        CONTRACT,
        preferred_element_type=jnp.float32,
    )
    grad_mixed = grad_mixed.astype(jnp.bfloat16).reshape(query_r.shape)
    attn_probs = attention_probs(query_r, key_r, segment)
    grad_value = jnp.einsum(
        "shqk,sqhd->skhd",
        attn_probs.astype(jnp.bfloat16),
        grad_mixed,
        preferred_element_type=jnp.float32,
    ).astype(jnp.bfloat16)
    grad_probs = jnp.einsum(
        "sqhd,skhd->shqk", grad_mixed, value_r, preferred_element_type=jnp.float32
    )
    grad_scores = attn_probs * (grad_probs - jnp.sum(attn_probs * grad_probs, -1, keepdims=True))
    grad_raw = (grad_scores * HEAD_DIM ** (-0.5)).astype(jnp.bfloat16)
    grad_query = jnp.einsum(
        "shqk,skhd->sqhd", grad_raw, key_r, preferred_element_type=jnp.float32
    ).astype(jnp.bfloat16)
    stacked = jnp.stack([grad_query.reshape(-1, MODEL_WIDTH), grad_value.reshape(-1, MODEL_WIDTH)])
    adapter_gradient = ADAPTER_SCALE * jnp.einsum(
        "krs,krd->ksd", reduced_gradients, stacked, preferred_element_type=jnp.float32
    )
    return (adapter_gradient, head_gradient)


def newton_schulz_orthogonal(moment):
    basis = moment / (jnp.sqrt(jnp.sum(moment * moment)) + 1e-07)
    for sweep in range(5):
        gram = jnp.dot(basis, basis.T, precision=TOP_PRECISION)
        poly = NS_B * gram + NS_C * jnp.dot(gram, gram, precision=TOP_PRECISION)
        basis = NS_A * basis + jnp.dot(poly, basis, precision=TOP_PRECISION)
    return basis


def local(
    input_token_ids,
    segments,
    labels,
    embedding,
    position_embedding_table,
    norm_gain_rows,
    norm_shift_rows,
    query_key_value_weight,
    attention_output_weight,
    attention_bias_stack,
    feedforward_in_weight,
    feedforward_bias,
    feedforward_out_weight,
    adapter_down_weight,
    adapter_up_weight,
    adapter_momentum,
    head,
    head_first_moment,
    head_second_moment,
):
    local_items = jnp.sum(jnp.max(segments, axis=-1) + 1).astype(jnp.float32)
    item_gradient_sum = lax.psum(local_items, ("dp", "tensor"))
    weight_list = (feedforward_in_weight, feedforward_bias, feedforward_out_weight)
    parameter_tree = (
        embedding,
        position_embedding_table,
        norm_gain_rows,
        norm_shift_rows,
        query_key_value_weight,
        attention_output_weight,
        attention_bias_stack,
        adapter_down_weight,
        adapter_up_weight.astype(jnp.bfloat16),
        head,
    )
    adapter_gradient_sum = jnp.zeros(adapter_up_weight.shape, jnp.float32)
    head_gradient_sum = jnp.zeros(head.shape, jnp.float32)
    loss_total = jnp.zeros((), jnp.float32)
    for micro_idx in range(input_token_ids.shape[0]):
        loss_piece, saved_activations = forward_layer(
            input_token_ids[micro_idx],
            segments[micro_idx],
            labels[micro_idx],
            parameter_tree,
            weight_list,
        )
        adapter_loss_piece, head_loss_piece = layer_backward_pass(
            saved_activations, parameter_tree, weight_list, item_gradient_sum
        )
        adapter_loss_piece, head_loss_piece, loss_piece = lax.psum(
            (adapter_loss_piece, head_loss_piece, loss_piece), ("dp", "tensor")
        )
        adapter_gradient_sum = adapter_gradient_sum + adapter_loss_piece
        head_gradient_sum = head_gradient_sum + head_loss_piece
        loss_total = loss_total + loss_piece
    global_gradient_norm = jnp.sqrt(
        jnp.sum(adapter_gradient_sum * adapter_gradient_sum)
        + jnp.sum(head_gradient_sum * head_gradient_sum)
    )
    scale_factor = jnp.minimum(1.0, CLIP_NORM / (global_gradient_norm + 1e-06))
    adapter_moment_next = ORTHO_MOMENTUM * adapter_momentum + scale_factor * adapter_gradient_sum
    orthogonal_update = jnp.stack(
        [
            newton_schulz_orthogonal(adapter_moment_next[0]),
            newton_schulz_orthogonal(adapter_moment_next[1]),
        ]
    )
    adapter_up_updated = adapter_up_weight - ORTHO_STEP_SIZE * orthogonal_update
    clipped = scale_factor * head_gradient_sum
    head_moment_next = BETA_ONE * head_first_moment + (1.0 - BETA_ONE) * clipped
    head_square_next = BETA_TWO * head_second_moment + (1.0 - BETA_TWO) * clipped * clipped
    first_hat = head_moment_next / (1.0 - BETA_ONE**STEP)
    second_hat = head_square_next / (1.0 - BETA_TWO**STEP)
    head_updated = head - ADAM_RATE * (first_hat / (jnp.sqrt(second_hat) + ADAM_EPS) + DECAY * head)
    return (
        loss_total,
        item_gradient_sum,
        global_gradient_norm,
        adapter_moment_next,
        adapter_up_updated,
        adapter_up_updated.astype(jnp.bfloat16),
        head_moment_next,
        head_square_next,
        head_updated,
        head_updated.astype(jnp.bfloat16),
    )


def solution(mesh):
    placed = (
        P(None, ("dp", "tensor"), None),
        P(None, ("dp", "tensor"), None),
        P(None, ("dp", "tensor"), None),
        P("tensor", None),
        P(),
        P(),
        P(),
        P(),
        P(),
        P(),
        P(None, "tensor"),
        P("tensor"),
        P("tensor", None),
        P(),
        P(),
        P(),
        P(),
        P(),
        P(),
    )
    return jax.shard_map(
        local,
        mesh=mesh,
        in_specs=placed,
        out_specs=(P(), P(), P(), P(), P(), P(), P(), P(), P(), P()),
        check_vma=False,
    )
```

profile of v0, /device:TPU:0, one launch (start us, length us, event | category | flops | bytes accessed | tf_op | source)
XLA Modules:
  0.0 1464.1 jit_solution(14740514176708388301)
XLA Ops:
  14.8 28.1 %copy.197 = bf16[192,50265]{0,1:T(8,128)(2,1)} copy(bf16[192,50265]{1,0:T(8,128)(2,1)} %param.26) | data formatting | bytes 38603520 | tf_op args[3]
  42.9 20.1 %gather_fusion.6 = bf16[2048,192]{1,0:T(8,128)(2,1)} fusion(bf16[192,50265]{0,1:T(8,128)(2,1)} %copy.197, s32[2048]{0:T(1024)S(1)} %fusion.317), kind=kCustom, calls=%fused_computation.4.clone | custom fusion | bytes 1581056 | tf_op jit(solution)/shard_map/jit(_take)/gather | solution.py:114
  71.7 12.7 all-gather.1
  119.3 21.3 %gather_fusion.2 = bf16[2048,192]{1,0:T(8,128)(2,1)} fusion(bf16[192,50265]{0,1:T(8,128)(2,1)} %copy.197, s32[2048]{0:T(1024)} %fusion.315), kind=kCustom, calls=%fused_computation.2.clone | custom fusion | bytes 1581056 | tf_op jit(solution)/shard_map/jit(_take)/gather | solution.py:114
  148.6 20.8 %gather_fusion.4 = bf16[2048,192]{1,0:T(8,128)(2,1)} fusion(bf16[192,50265]{0,1:T(8,128)(2,1)} %copy.197, s32[2048]{0:T(1024)} %fusion.316), kind=kCustom, calls=%fused_computation.3.clone | custom fusion | bytes 1581056 | tf_op jit(solution)/shard_map/jit(_take)/gather | solution.py:114
  175.0 20.8 %gather_fusion = bf16[2048,192]{1,0:T(8,128)(2,1)} fusion(bf16[192,50265]{0,1:T(8,128)(2,1)} %copy.197, s32[2048]{0:T(1024)} %fusion.314), kind=kCustom, calls=%fused_computation.clone | custom fusion | bytes 1581056 | tf_op jit(solution)/shard_map/jit(_take)/gather | solution.py:114
  461.4 29.2 %all-gather.17.cloned.1.call-done = bf16[2048,768]{1,0:T(8,128)(2,1)} async-done(((bf16[512,768]{1,0:T(8,128)(2,1)}), bf16[2048,768]{1,0:T(8,128)(2,1)}) %all-gather.17.cloned.1.call-update) | async-done | bytes 3145744 | tf_op jit(solution)/shard_map/all_gather | solution.py:65
  497.7 23.0 %all-gather.15.cloned.1.call-done = bf16[2048,768]{1,0:T(8,128)(2,1)} async-done(((bf16[512,768]{1,0:T(8,128)(2,1)}), bf16[2048,768]{1,0:T(8,128)(2,1)}) %all-gather.15.cloned.1.call-update) | async-done | bytes 3145744 | tf_op jit(solution)/shard_map/all_gather | solution.py:65
  527.8 23.0 %all-gather.19.cloned.1.call-done = bf16[2048,768]{1,0:T(8,128)(2,1)} async-done(((bf16[512,768]{1,0:T(8,128)(2,1)}), bf16[2048,768]{1,0:T(8,128)(2,1)}) %all-gather.19.cloned.1.call-update) | async-done | bytes 3145744 | tf_op jit(solution)/shard_map/all_gather | solution.py:65
  550.9 44.4 %fusion.39 = (f32[2048,768]{1,0:T(8,128)S(1)}, f32[2048,768]{1,0:T(8,128)}, f32[2048,768]{1,0:T(8,128)}, f32[2048,768]{1,0:T(8,128)S(1)}) fusion(f32[768]{0:T(1024)S(1)} %convert_element_type.473, f32[2048,768]{1,0:T(8,128)} %fusion.425, f32[2048,768]{1,0:T(8,128)} %fusion.423, bf16[2048,768]{1,0:T(8,128)(2,1)} %all-gather.19.cloned.1.call-done, ...), kind=kOutput, calls=%fused_computation.51 | convolution fusion | flops 2713190400 | bytes 42077184 | tf_op jit(solution)/shard_map/dot_general | solution.py:64
  604.4 11.0 fusion.77
  628.3 39.4 %psum.95 = f32[]{:T(128)} all-reduce(f32[]{:T(128)S(6)} %convert_element_type.532), channel_id=1, replica_groups=mesh['dp'=8,'tensor'=4] {'dp','tensor'}, use_global_device_ids=true, to_apply=%region_58.61 | all-reduce | flops 1 | bytes 8 | tf_op jit(solution)/shard_map/psum | solution.py:295
  686.8 37.9 %reduce-scatter.11.cloned.1.call-done = f32[512,768]{1,0:T(8,128)} async-done(((f32[2048,768]{1,0:T(8,128)}), f32[512,768]{1,0:T(8,128)}) %reduce-scatter.11.cloned.1.call-update) | async-done | bytes 1572880 | tf_op jit(solution)/shard_map/reduce_scatter | solution.py:72
  724.7 60.8 %reduce-scatter.13.cloned.1.call-done = f32[512,768]{1,0:T(8,128)} async-done(((f32[2048,768]{1,0:T(8,128)}), f32[512,768]{1,0:T(8,128)}) %reduce-scatter.13.cloned.1.call-update) | async-done | bytes 1572880 | tf_op jit(solution)/shard_map/reduce_scatter | solution.py:72
  828.8 12.7 fusion.107
  841.7 17.4 %all-gather.25.cloned.1.call-done = bf16[2048,768]{1,0:T(8,128)(2,1)} async-done(((bf16[512,768]{1,0:T(8,128)(2,1)}), bf16[2048,768]{1,0:T(8,128)(2,1)}) %all-gather.25.cloned.1.call-update) | async-done | bytes 3145744 | tf_op jit(solution)/shard_map/all_gather | solution.py:84
  859.1 12.8 fusion.106
  872.3 16.9 %all-gather.23.cloned.1.call-done = bf16[2048,768]{1,0:T(8,128)(2,1)} async-done(((bf16[512,768]{1,0:T(8,128)(2,1)}), bf16[2048,768]{1,0:T(8,128)(2,1)}) %all-gather.23.cloned.1.call-update) | async-done | bytes 3145744 | tf_op jit(solution)/shard_map/all_gather | solution.py:84
  889.3 12.7 fusion.105
  902.1 17.2 %all-gather.13.cloned.1.call-done = bf16[2048,768]{1,0:T(8,128)(2,1)} async-done(((bf16[512,768]{1,0:T(8,128)(2,1)}), bf16[2048,768]{1,0:T(8,128)(2,1)}) %all-gather.13.cloned.1.call-update) | async-done | bytes 3145744 | tf_op jit(solution)/shard_map/all_gather | solution.py:65
  919.3 16.7 %fusion.36 = (f32[2048,768]{1,0:T(8,128)S(1)}, f32[2048,768]{1,0:T(8,128)S(1)}) fusion(f32[768]{0:T(1024)S(1)} %convert_element_type.473, bf16[2048,768]{1,0:T(8,128)(2,1)} %all-gather.13.cloned.1.call-done, bf16[768,768]{1,0:T(8,128)(2,1)} %param.33), kind=kOutput, calls=%fused_computation.48 | convolution fusion | flops 2515009536 | bytes 16911360 | tf_op jit(solution)/shard_map/dot_general | solution.py:64
  947.0 33.4 %reduce-scatter.23.cloned.1.call-done = f32[512,768]{1,0:T(8,128)} async-done(((f32[2048,768]{1,0:T(8,128)}), f32[512,768]{1,0:T(8,128)}) %reduce-scatter.23.cloned.1.call-update) | async-done | bytes 1572880 | tf_op jit(solution)/shard_map/reduce_scatter | solution.py:90
  980.4 60.8 %reduce-scatter.21.cloned.1.call-done = f32[512,768]{1,0:T(8,128)} async-done(((f32[2048,768]{1,0:T(8,128)}), f32[512,768]{1,0:T(8,128)}) %reduce-scatter.21.cloned.1.call-update) | async-done | bytes 1572880 | tf_op jit(solution)/shard_map/reduce_scatter | solution.py:90
  1041.2 61.1 %reduce-scatter.19.cloned.1.call-done = f32[512,768]{1,0:T(8,128)} async-done(((f32[2048,768]{1,0:T(8,128)}), f32[512,768]{1,0:T(8,128)}) %reduce-scatter.19.cloned.1.call-update) | async-done | bytes 1572880 | tf_op jit(solution)/shard_map/reduce_scatter | solution.py:90
  1108.6 54.5 %reduce-scatter.9.cloned.1.call-done = f32[512,768]{1,0:T(8,128)} async-done(((f32[2048,768]{1,0:T(8,128)}), f32[512,768]{1,0:T(8,128)}) %reduce-scatter.9.cloned.1.call-update) | async-done | bytes 1572880 | tf_op jit(solution)/shard_map/reduce_scatter | solution.py:72
  1177.2 28.5 %all-gather.21.cloned.1.call-done = bf16[2048,768]{1,0:T(8,128)(2,1)} async-done(((bf16[512,768]{1,0:T(8,128)(2,1)}), bf16[2048,768]{1,0:T(8,128)(2,1)}) %all-gather.21.cloned.1.call-update) | async-done | bytes 3145744 | tf_op jit(solution)/shard_map/all_gather | solution.py:84
  1205.7 12.7 fusion.104
  1247.1 18.8 %fusion.170 = bf16[12,64,512]{2,1,0:T(8,128)(2,1)} fusion(bf16[512,12,64]{0,2,1:T(8,128)(2,1)} %get-tuple-element.106, f32[12,512,512]{1,2,0:T(8,128)} %fusion.428, f32[12,512,512]{1,2,0:T(8,128)} %get-tuple-element.149, f32[12,512]{1,0:T(8,128)S(1)} %copy-done.239), kind=kOutput, calls=%fused_computation.298 | convolution fusion | flops 425073152 | bytes 26763264 | tf_op jit(solution)/shard_map/shqk,skhd->sqhd/dot_general | solution.py:254
  1333.1 17.6 %fusion.173 = bf16[12,64,512]{2,1,0:T(8,128)(2,1)S(1)} fusion(bf16[512,12,64]{0,2,1:T(8,128)(2,1)S(1)} %copy-done.82, f32[12,512,512]{1,2,0:T(8,128)} %fusion.427, f32[12,512,512]{1,2,0:T(8,128)} %get-tuple-element.158, f32[12,512]{1,0:T(8,128)S(1)} %copy-done.241), kind=kOutput, calls=%fused_computation.299 | convolution fusion | flops 425073152 | bytes 26763264 | tf_op jit(solution)/shard_map/shqk,skhd->sqhd/dot_general | solution.py:254
  1352.1 17.8 %fusion.167 = bf16[12,64,512]{2,1,0:T(8,128)(2,1)S(1)} fusion(bf16[512,12,64]{0,2,1:T(8,128)(2,1)} %get-tuple-element.107, f32[12,512,512]{1,2,0:T(8,128)} %fusion.429, f32[12,512,512]{1,2,0:T(8,128)} %get-tuple-element.153, f32[12,512]{1,0:T(8,128)S(1)} %copy-done.237), kind=kOutput, calls=%fused_computation.297 | convolution fusion | flops 425073152 | bytes 26763264 | tf_op jit(solution)/shard_map/shqk,skhd->sqhd/dot_general | solution.py:254
  1372.3 18.4 %fusion.164 = bf16[12,64,512]{2,1,0:T(8,128)(2,1)} fusion(bf16[512,12,64]{0,2,1:T(8,128)(2,1)S(1)} %copy-done.80, f32[12,512,512]{1,2,0:T(8,128)} %fusion.430, f32[12,512,512]{1,2,0:T(8,128)} %get-tuple-element.145, f32[12,512]{1,0:T(8,128)S(1)} %copy-done.235), kind=kOutput, calls=%fused_computation.296 | convolution fusion | flops 425073152 | bytes 26763264 | tf_op jit(solution)/shard_map/shqk,skhd->sqhd/dot_general | solution.py:254
  1398.1 40.3 %all-reduce = (f32[]{:T(128)}, f32[2,8,768]{2,1,0:T(8,128)}, f32[769]{0:T(1024)S(1)}) all-reduce(f32[]{:T(128)S(6)} %add.806, f32[2,8,768]{2,1,0:T(8,128)} %fusion.211, f32[769]{0:T(1024)S(1)} %copy-done.173), channel_id=1, replica_groups=mesh['dp'=8,'tensor'=4] {'dp','tensor'}, use_global_device_ids=true, to_apply=%region_13.16 | all-reduce | flops 13058 | bytes 104464 | tf_op jit(solution)/shard_map/psum | solution.py:323
  (831 shorter events, 576.9 us)
Async XLA Ops:
  7.2 275.7 %copy-start = (bf16[3,768,768]{2,1,0:T(8,128)(2,1)S(1)}, bf16[3,768,768]{2,1,0:T(8,128)(2,1)}, u32[]{:S(2)}) copy-start(bf16[3,768,768]{2,1,0:T(8,128)(2,1)} %param.30) | copy-start | bytes 10616836
  67.4 165.7 %all-to-all-start.3 = ((bf16[192,4,512]{2,0,1:T(8,128)(2,1)}), bf16[192,4,512]{2,0,1:T(8,128)(2,1)}, u32[]{:S(2)}, u32[]{:S(2)}) async-start(bf16[192,4,512]{2,0,1:T(8,128)(2,1)} %copy.225), calls=%async_computation.6 | async-start | bytes 1572864 | tf_op jit(solution)/shard_map/all_to_all | solution.py:115
  101.1 130.1 %copy-start.108 = (s32[1,1,512]{2,1,0:T(1,128)}, s32[1,1,512]{2,1,0:T(1,128)S(1)}, u32[]{:S(2)}) copy-start(s32[1,1,512]{2,1,0:T(1,128)S(1)} %get-tuple-element.129) | copy-start | bytes 6148
  101.2 131.1 %copy-start.110 = (s32[1,1,512]{2,1,0:T(1,128)}, s32[1,1,512]{2,1,0:T(1,128)S(1)}, u32[]{:S(2)}) copy-start(s32[1,1,512]{2,1,0:T(1,128)S(1)} %get-tuple-element.128) | copy-start | bytes 6148
  231.3 223.3 %copy-start.133 = (f32[768]{0:T(1024)}, f32[768]{0:T(1024)S(1)}, u32[]{:S(2)}) copy-start(f32[768]{0:T(1024)S(1)} %get-tuple-element.20) | copy-start | bytes 9220
  231.3 224.9 %copy-start.90 = (f32[768]{0:T(1024)}, f32[768]{0:T(1024)S(1)}, u32[]{:S(2)}) copy-start(f32[768]{0:T(1024)S(1)} %get-tuple-element.21) | copy-start | bytes 9220
  233.1 15.9 %all-to-all-start.1 = ((bf16[192,4,512]{2,0,1:T(8,128)(2,1)}), bf16[192,4,512]{2,0,1:T(8,128)(2,1)}, u32[]{:S(2)}, u32[]{:S(2)}) async-start(bf16[192,4,512]{2,0,1:T(8,128)(2,1)} %copy.207), calls=%async_computation.2 | async-start | bytes 1572864 | tf_op jit(solution)/shard_map/all_to_all | solution.py:115
  249.0 15.9 %all-to-all-start.2 = ((bf16[192,4,512]{2,0,1:T(8,128)(2,1)}), bf16[192,4,512]{2,0,1:T(8,128)(2,1)}, u32[]{:S(2)}, u32[]{:S(2)}) async-start(bf16[192,4,512]{2,0,1:T(8,128)(2,1)} %copy.216), calls=%async_computation.4 | async-start | bytes 1572864 | tf_op jit(solution)/shard_map/all_to_all | solution.py:115
  265.0 32.3 %all-to-all-start = ((bf16[192,4,512]{2,0,1:T(8,128)(2,1)}), bf16[192,4,512]{2,0,1:T(8,128)(2,1)}, u32[]{:S(2)}, u32[]{:S(2)}) async-start(bf16[192,4,512]{2,0,1:T(8,128)(2,1)} %copy.198), calls=%async_computation | async-start | bytes 1572864 | tf_op jit(solution)/shard_map/all_to_all | solution.py:115
  269.2 221.4 %all-gather.17.cloned.1.call-start = ((), (), s32[]{:S(2)}) async-start(), calls=%async_computation.16 | async-start | bytes 3932160 | tf_op jit(solution)/shard_map/all_gather | solution.py:65
  459.8 60.9 %all-gather.15.cloned.1.call-start = ((), (), s32[]{:S(2)}) async-start(), calls=%async_computation.14 | async-start | bytes 3932160 | tf_op jit(solution)/shard_map/all_gather | solution.py:65
  460.6 90.3 %all-gather.19.cloned.1.call-start = ((), (), s32[]{:S(2)}) async-start(), calls=%async_computation.18 | async-start | bytes 3932160 | tf_op jit(solution)/shard_map/all_gather | solution.py:65
  461.3 225.5 %reduce-scatter.15.cloned.1.call-start = ((), (), s32[]{:S(2)}) async-start(), calls=%async_computation.19 | async-start | bytes 7864320 | tf_op jit(solution)/shard_map/reduce_scatter | solution.py:72
  604.4 120.4 %reduce-scatter.11.cloned.1.call-start = ((), (), s32[]{:S(2)}) async-start(), calls=%async_computation.15 | async-start | bytes 7864320 | tf_op jit(solution)/shard_map/reduce_scatter | solution.py:72
  615.4 170.1 %reduce-scatter.13.cloned.1.call-start = ((), (), s32[]{:S(2)}) async-start(), calls=%async_computation.17 | async-start | bytes 7864320 | tf_op jit(solution)/shard_map/reduce_scatter | solution.py:72
  626.2 202.7 %all-gather.27.cloned.1.call-start = ((), (), s32[]{:S(2)}) async-start(), calls=%async_computation.26 | async-start | bytes 3932160 | tf_op jit(solution)/shard_map/all_gather | solution.py:84
  668.2 125.2 %copy-start.96 = (f32[768,1]{0,1:T(1,128)}, f32[768,1]{0,1:T(1,128)S(1)}, u32[]{:S(2)}) copy-start(f32[768,1]{0,1:T(1,128)S(1)} %reshape.1910) | copy-start | bytes 9220
  684.0 101.5 %copy-start.5 = (f32[512,768]{1,0:T(8,128)S(1)}, f32[512,768]{1,0:T(8,128)}, u32[]{:S(2)}) copy-start(f32[512,768]{1,0:T(8,128)} %copy-done.4) | copy-start | bytes 4718596
  684.0 101.5 %copy-start.130 = (f32[768]{0:T(1024)S(1)}, f32[768]{0:T(1024)}, u32[]{:S(2)}) copy-start(f32[768]{0:T(1024)} %get-tuple-element.14) | copy-start | bytes 9220
  684.1 101.5 %copy-start.141 = (f32[512]{0:T(512)S(1)}, f32[512]{0:T(512)}, u32[]{:S(2)}) copy-start(f32[512]{0:T(512)} %copy-done.140) | copy-start | bytes 6148
  685.4 106.3 %copy-start.118 = (f32[512]{0:T(512)}, f32[512]{0:T(512)S(1)}, u32[]{:S(2)}) copy-start(f32[512]{0:T(512)S(1)} %broadcast_multiply_fusion.10) | copy-start | bytes 6148
  686.8 104.9 %copy-start.158 = (f32[512]{0:T(512)}, f32[512]{0:T(512)S(1)}, u32[]{:S(2)}) copy-start(f32[512]{0:T(512)S(1)} %multiply_reduce_fusion.22) | copy-start | bytes 6148
  686.8 104.8 %copy-start.150 = (f32[512]{0:T(512)}, f32[512]{0:T(512)S(1)}, u32[]{:S(2)}) copy-start(f32[512]{0:T(512)S(1)} %fusion.329) | copy-start | bytes 6148
  800.2 58.9 %all-gather.25.cloned.1.call-start = ((), (), s32[]{:S(2)}) async-start(), calls=%async_computation.24 | async-start | bytes 3932160 | tf_op jit(solution)/shard_map/all_gather | solution.py:84
  810.9 78.3 %all-gather.23.cloned.1.call-start = ((), (), s32[]{:S(2)}) async-start(), calls=%async_computation.22 | async-start | bytes 3932160 | tf_op jit(solution)/shard_map/all_gather | solution.py:84
  822.3 97.0 %all-gather.13.cloned.1.call-start = ((), (), s32[]{:S(2)}) async-start(), calls=%async_computation.12 | async-start | bytes 3932160 | tf_op jit(solution)/shard_map/all_gather | solution.py:65
  822.9 157.5 %reduce-scatter.23.cloned.1.call-start = ((), (), s32[]{:S(2)}) async-start(), calls=%async_computation.27 | async-start | bytes 7864320 | tf_op jit(solution)/shard_map/reduce_scatter | solution.py:90
  841.6 199.6 %reduce-scatter.21.cloned.1.call-start = ((), (), s32[]{:S(2)}) async-start(), calls=%async_computation.25 | async-start | bytes 7864320 | tf_op jit(solution)/shard_map/reduce_scatter | solution.py:90
  871.9 230.4 %reduce-scatter.19.cloned.1.call-start = ((), (), s32[]{:S(2)}) async-start(), calls=%async_computation.23 | async-start | bytes 7864320 | tf_op jit(solution)/shard_map/reduce_scatter | solution.py:90
  902.0 261.1 %reduce-scatter.9.cloned.1.call-start = ((), (), s32[]{:S(2)}) async-start(), calls=%async_computation.13 | async-start | bytes 7864320 | tf_op jit(solution)/shard_map/reduce_scatter | solution.py:72
  945.1 260.6 %all-gather.21.cloned.1.call-start = ((), (), s32[]{:S(2)}) async-start(), calls=%async_computation.20 | async-start | bytes 3932160 | tf_op jit(solution)/shard_map/all_gather | solution.py:84
  1177.0 100.0 %reduce-scatter.17.cloned.1.call-start = ((), (), s32[]{:S(2)}) async-start(), calls=%async_computation.21 | async-start | bytes 7864320 | tf_op jit(solution)/shard_map/reduce_scatter | solution.py:90
  (230 other events, 2532.5 us)
Sparse Core Ops, SparseCore 0:
  460.0 30.5 all-gather.16
  492.1 28.5 all-gather.14
  522.3 28.5 all-gather.18
  604.5 59.1 reduce-scatter.14
  666.2 58.4 reduce-scatter.10
  727.1 58.3 reduce-scatter.12
  800.3 28.5 all-gather.26
  830.5 28.5 all-gather.24
  860.7 28.5 all-gather.22
  890.7 28.5 all-gather.12
  922.0 58.3 reduce-scatter.22
  982.8 58.3 reduce-scatter.20
  1043.9 58.3 reduce-scatter.18
  1104.7 58.3 reduce-scatter.8
  1177.1 28.5 all-gather.20
  1218.5 58.3 reduce-scatter.16
where the time goes:
time: 1480 us; the launch traced here: 1460 us
  waiting for transfers between devices  480 us (32%)
  matrix products  419 us (28%)
  local copies, waits for them, and re-layouts  275 us (19%)
  other arithmetic  139 us (9%)
  blocking collectives  109 us (7%)
  between operations  24.4 us (2%)
  starting transfers between devices  18.4 us (1%)
    reduce_scatter x4, waiting for transfers between devices, ffn_backward(): lax.psum_scatter(lax.dot_general(grad_pre, input_weight, CONTRACT, prefer...  158 us
    reduce_scatter x4, waiting for transfers between devices, ffn_forward(): lax.psum_scatter(jnp.dot(act_r, output_weight, preferred_element_type=jnp...  153 us
    all_gather x4, waiting for transfers between devices, ffn_forward(): lax.all_gather(normed1_r, 'tensor', axis=0, tiled=True)  92.5 us
    gather x4, local copies, waits for them, and re-layouts, forward_layer(): picked = jnp.take(embedding, all_ids.reshape(-1), axis=1)  82.9 us
    dot_general x4, matrix products, ffn_forward(): jnp.dot(lax.all_gather(normed1_r, 'tensor', axis=0, tiled=True), input_we...  75.3 us
    dot_general x4, matrix products, layer_backward_pass(): jnp.einsum('shqk,skhd->sqhd', grad_raw, key_r, preferred_element_type=jnp...  72.6 us
    all_gather x4, waiting for transfers between devices, ffn_backward(): lax.all_gather(grad_r, 'tensor', axis=0, tiled=True)  68.7 us
    unnamed x485, local copies, waits for them, and re-layouts  60.3 us
  transfers between devices with their start and end apart: 20, of which 17 were waited for; matrix products, arithmetic and copies ran while one was open for 26% of the time, Pallas kernels for 0%

commit v1 on v0

v1 whole, which is shorter than its diff:
```python
import functools
import math

import jax
import jax.numpy as jnp
from jax import lax
from jax.experimental import pallas as pl
from jax.experimental.pallas import tpu as pltpu
from jax.sharding import PartitionSpec as P

HEAD_DIM = 64
STEP = 10
LN_EPS = 1e-05
CLIP_NORM = 0.5
ORTHO_MOMENTUM = 0.5
ORTHO_STEP_SIZE = 1.0
NS_A = 3.4445
NS_B = -4.775
NS_C = 2.0315
BETA_ONE = 0.9
BETA_TWO = 0.999
ADAM_RATE = 0.05
ADAM_EPS = 1e-08
DECAY = 0.01
TOP_PRECISION = lax.Precision.HIGHEST

F32 = jnp.float32
BF16 = jnp.bfloat16
LANES = 128
GROUP = 256
BLOCK = 128
NN = (((1,), (0,)), ((), ()))
NT = (((1,), (1,)), ((), ()))
TN = (((0,), (0,)), ((), ()))
INV_SQRT2 = 1.0 / math.sqrt(2.0)
INV_SQRT_2PI = 1.0 / math.sqrt(2.0 * math.pi)


def mm(left, right, dims=NN):
    return lax.dot_general(left, right, dims, preferred_element_type=F32)


def row_mean(rows):
    return jnp.mean(rows, axis=-1, keepdims=True)


def layer_kernel(
    x_ref,
    seg_ref,
    label_ref,
    pos_ref,
    gain_ref,
    shift_ref,
    bias_ref,
    down_ref,
    up_ref,
    head_ref,
    ffb_ref,
    acc_in_ref,
    wqkv_hbm,
    wo_hbm,
    win_hbm,
    wout_hbm,
    acc_ref,
    wqkv,
    wo,
    win,
    wout,
    xb,
    normed0,
    q,
    k,
    v,
    red,
    vr,
    pr,
    probs,
    mixed,
    xh1,
    stat1,
    acc,
    slope,
    act,
    sems,
):
    rows, width = normed0.shape
    parts = x_ref.shape[0]
    hidden_part = win.shape[2]
    groups = width // GROUP
    per_group = GROUP // HEAD_DIM
    blocks = rows // BLOCK
    tiles = rows // GROUP
    span = 3 * BLOCK
    chunk = 256 if hidden_part % 256 == 0 else hidden_part
    step_rows = 64
    row_steps = rows // step_rows

    copies = [
        pltpu.make_async_copy(wqkv_hbm, wqkv, sems.at[0]),
        pltpu.make_async_copy(wo_hbm, wo, sems.at[1]),
        pltpu.make_async_copy(win_hbm, win, sems.at[2]),
        pltpu.make_async_copy(wout_hbm, wout, sems.at[3]),
    ]
    for copy in copies:
        copy.start()

    seg_row = seg_ref[...].astype(F32)
    lane = lax.broadcasted_iota(jnp.int32, (rows, rows), 1)
    sub = lax.broadcasted_iota(jnp.int32, (rows, rows), 0)
    seg_col = jnp.sum(jnp.where(lane == sub, seg_row, 0.0), axis=1, keepdims=True)
    same = seg_col == seg_row
    place = jnp.sum(jnp.where(same & (lane < sub), 1.0, 0.0), axis=1, keepdims=True)
    one_hot = jnp.where(lane == place.astype(jnp.int32), 1.0, 0.0).astype(BF16)
    pieces = jnp.concatenate([x_ref[t] for t in range(parts)], axis=1).astype(F32)
    acc[...] = pieces + mm(one_hot, pos_ref[...])

    gain0, gain1, gain2 = gain_ref[0:1], gain_ref[1:2], gain_ref[2:3]
    shift0, shift1, shift2 = shift_ref[0:1], shift_ref[1:2], shift_ref[2:3]

    def at(i):
        return pl.ds(pl.multiple_of(i * step_rows, step_rows), step_rows)

    def norm0(i, carry):
        x = acc[at(i), :]
        off = x - row_mean(x)
        y = off * lax.rsqrt(row_mean(off * off) + LN_EPS) * gain0 + shift0
        normed0[at(i), :] = y
        xb[at(i), :] = y.astype(BF16)
        return carry

    lax.fori_loop(0, row_steps, norm0, 0)

    red[...] = mm(xb[...], down_ref[...]).astype(BF16)
    copies[0].wait()
    q[...] = (
        (mm(xb[...], wqkv[0]) + bias_ref[0:1] + mm(red[...], up_ref[0])).astype(BF16)
        * BF16(HEAD_DIM**-0.5)
    )
    k[...] = (mm(xb[...], wqkv[1]) + bias_ref[1:2]).astype(BF16)
    v[...] = (mm(xb[...], wqkv[2]) + bias_ref[2:3] + mm(red[...], up_ref[1])).astype(BF16)

    head_of = lax.broadcasted_iota(jnp.int32, (1, GROUP), 1) // HEAD_DIM
    in_head = [head_of == h for h in range(per_group)]
    keep = [jnp.where(m, 1.0, 0.0).astype(BF16) for m in in_head]

    def mask_block(b, c):
        hit = seg_col[b * BLOCK : (b + 1) * BLOCK] == seg_row[:, c * BLOCK : (c + 1) * BLOCK]
        return jnp.where(hit, 0.0, -1e9)

    away = {
        (b, c): mask_block(b, c)
        for b in range(blocks)
        for c in range(max(b - 1, 0), min(b + 2, blocks))
    }

    def tile_rows(t):
        lo = min(max(2 * t - 1, 0) * BLOCK, rows - min(span, rows))
        hi = min((2 * t + 3) * BLOCK, rows)
        return lo, hi

    def block_pieces(b):
        first, last = max(b - 1, 0), min(b + 1, blocks - 1)
        found = []
        for t in range(tiles):
            lo, hi = max(first, 2 * t), min(last, 2 * t + 1)
            if lo <= hi:
                found.append((t, lo, hi))
        return found

    zero_block = jnp.zeros((BLOCK, BLOCK), BF16)

    def spread(values, t, lo, hi):
        parts_ = [values] if lo == 2 * t else [zero_block, values]
        if hi == 2 * t:
            parts_.append(zero_block)
        return parts_[0] if len(parts_) == 1 else jnp.concatenate(parts_, axis=1)

    def attention(g, carry):
        lanes = pl.ds(pl.multiple_of(g * GROUP, GROUP), GROUP)
        qg, kg, vg = q[:, lanes], k[:, lanes], v[:, lanes]
        scores = []
        for t in range(tiles):
            lo, hi = tile_rows(t)
            stack = jnp.concatenate([qg[lo:hi] * keep[h] for h in range(per_group)], axis=0)
            scores.append(mm(stack, kg[t * GROUP : (t + 1) * GROUP], NT))
        out = jnp.zeros((rows, GROUP), F32)
        low = jnp.zeros((rows, GROUP), F32)
        for h in range(per_group):
            vrh = vg * keep[h] + red[...] * (1 - keep[h])
            prob_tiles = [[] for _ in range(tiles)]
            for b in range(blocks):
                found = []
                for t, lo, hi in block_pieces(b):
                    first, last = tile_rows(t)
                    top = h * (last - first) + b * BLOCK - first
                    s = scores[t][top : top + BLOCK, (lo - 2 * t) * BLOCK : (hi + 1 - 2 * t) * BLOCK]
                    far = jnp.concatenate([away[b, c] for c in range(lo, hi + 1)], axis=1)
                    found.append(s + far)
                peak = functools.reduce(
                    jnp.maximum, [jnp.max(s, axis=1, keepdims=True) for s in found]
                )
                found = [jnp.exp(s - peak) for s in found]
                total = functools.reduce(
                    jnp.add, [jnp.sum(s, axis=1, keepdims=True) for s in found]
                )
                inv = 1.0 / total
                for (t, lo, hi), s in zip(block_pieces(b), found):
                    prob_tiles[t].append(spread((s * inv).astype(BF16), t, lo, hi))
            res = [None] * blocks
            for t in range(tiles):
                first, last = tile_rows(t)
                pt = jnp.concatenate(prob_tiles[t], axis=0)
                probs[g * per_group + h, t, 0 : last - first, :] = pt
                part = mm(pt, vrh[t * GROUP : (t + 1) * GROUP])
                for i in range((last - first) // BLOCK):
                    b = first // BLOCK + i
                    piece = part[i * BLOCK : (i + 1) * BLOCK]
                    res[b] = piece if res[b] is None else res[b] + piece
            res = jnp.concatenate(res, axis=0)
            out = jnp.where(in_head[h], res, out)
            low = jnp.where(in_head[(h + 1) % per_group], res, low)
        mixed[:, lanes] = out.astype(BF16)
        pr[:, lanes] = low.astype(BF16)
        return carry

    lax.fori_loop(0, groups, attention, 0)

    copies[1].wait()
    acc[...] = mm(mixed[...], wo[...]) + bias_ref[3:4]

    def norm1(i, carry):
        x = normed0[at(i), :] + acc[at(i), :]
        off = x - row_mean(x)
        inv = lax.rsqrt(row_mean(off * off) + LN_EPS)
        xh = off * inv
        xh1[at(i), :] = xh
        stat1[at(i), :] = inv
        xb[at(i), :] = (xh * gain1 + shift1).astype(BF16)
        return carry

    lax.fori_loop(0, row_steps, norm1, 0)

    copies[2].wait()
    for t in range(parts):
        for c in range(0, hidden_part, chunk):
            at_hidden = slice(t * hidden_part + c, t * hidden_part + c + chunk)
            pre = mm(xb[...], win[t, :, c : c + chunk]) + ffb_ref[:, at_hidden]
            phi = 0.5 + 0.5 * lax.erf(pre * INV_SQRT2)
            act[:, at_hidden] = (pre * phi).astype(BF16)
            slope[:, at_hidden] = phi + pre * jnp.exp(-0.5 * pre * pre) * INV_SQRT_2PI
    copies[3].wait()
    for n in range(0, width, GROUP):
        acc[:, n : n + GROUP] = mm(act[...], wout[:, n : n + GROUP])

    head = head_ref[0:1, 0:width]
    head_bias = head_ref[0:1, width : width + 1]
    hg = head * gain2
    hg_mean = row_mean(hg)
    bias4 = bias_ref[4:5]
    base = jnp.sum(shift2 * head, axis=1, keepdims=True)

    inv_cols = []
    dot_cols = []
    for i in range(row_steps):
        part = slice(i * step_rows, (i + 1) * step_rows)
        x = xh1[part, :] * gain1 + shift1 + (acc[part, :] + bias4)
        off = x - row_mean(x)
        inv = lax.rsqrt(row_mean(off * off) + LN_EPS)
        xh = off * inv
        acc[part, :] = xh
        inv_cols.append(inv)
        dot_cols.append(jnp.sum(xh * hg, axis=1, keepdims=True))
    inv2 = jnp.concatenate(inv_cols, axis=0)
    dots = jnp.concatenate(dot_cols, axis=0)

    slots = label_ref.shape[1]
    slot = lax.broadcasted_iota(jnp.int32, (rows, slots), 1).astype(F32)
    member = jnp.where(seg_col == slot, 1.0, 0.0)
    counts = jnp.sum(member, axis=0, keepdims=True)
    sums = jnp.sum(member * (dots + base), axis=0, keepdims=True)
    most = jnp.maximum(counts, 1.0)
    error = jnp.where(counts > 0, sums / most + head_bias - label_ref[...], 0.0)
    grad_pred = 2.0 * error
    weight = jnp.sum(member * (grad_pred / most), axis=1, keepdims=True)
    loss = jnp.sum(error * error, axis=1, keepdims=True)
    weight_sum = jnp.sum(grad_pred, axis=1, keepdims=True)
    items = jnp.max(seg_row, axis=1, keepdims=True) + 1.0

    head_grad = jnp.zeros((8, width), F32)
    for i in range(row_steps):
        part = slice(i * step_rows, (i + 1) * step_rows)
        xh = acc[part, :]
        w = weight[part]
        weighted = xh * w
        for j in range(step_rows // 8):
            head_grad = head_grad + weighted[j * 8 : (j + 1) * 8]
        grad = (inv2[part] * w) * (hg - hg_mean - xh * (dots[part] * (1.0 / width)))
        acc[part, :] = grad
        xb[part, :] = grad.astype(BF16)
    head_grad = jnp.sum(head_grad, axis=0, keepdims=True) * gain2 + weight_sum * shift2

    for t in range(parts):
        for c in range(0, hidden_part, chunk):
            at_hidden = slice(t * hidden_part + c, t * hidden_part + c + chunk)
            back = mm(xb[...], wout[at_hidden, :], NT)
            act[:, at_hidden] = (back * slope[:, at_hidden]).astype(BF16)
    for n in range(0, width, GROUP):
        total = acc[:, n : n + GROUP]
        for t in range(parts):
            total = total + mm(
                act[:, t * hidden_part : (t + 1) * hidden_part], win[t, n : n + GROUP, :], NT
            )
        acc[:, n : n + GROUP] = total

    def back1(i, carry):
        g = acc[at(i), :] * gain1
        xh = xh1[at(i), :]
        grad = stat1[at(i), :] * (g - row_mean(g) - xh * row_mean(g * xh))
        xb[at(i), :] = grad.astype(BF16)
        return carry

    lax.fori_loop(0, row_steps, back1, 0)

    mixed[...] = mm(xb[...], wo[...], NT).astype(BF16)

    def attention_back(g, carry):
        lanes = pl.ds(pl.multiple_of(g * GROUP, GROUP), GROUP)
        gg, kg, vg = mixed[:, lanes], k[:, lanes], v[:, lanes]
        grads = []
        for t in range(tiles):
            lo, hi = tile_rows(t)
            stack = jnp.concatenate([gg[lo:hi] * keep[h] for h in range(per_group)], axis=0)
            grads.append(mm(stack, vg[t * GROUP : (t + 1) * GROUP], NT))
        out = jnp.zeros((rows, GROUP), F32)
        for h in range(per_group):
            score_tiles = [[] for _ in range(tiles)]
            for b in range(blocks):
                found = []
                for t, lo, hi in block_pieces(b):
                    first, last = tile_rows(t)
                    top = b * BLOCK - first
                    lane_at = slice((lo - 2 * t) * BLOCK, (hi + 1 - 2 * t) * BLOCK)
                    dp = grads[t][h * (last - first) + top : h * (last - first) + top + BLOCK, lane_at]
                    p = probs[g * per_group + h, t, top : top + BLOCK, lane_at].astype(F32)
                    found.append((p, dp))
                shared = functools.reduce(
                    jnp.add, [jnp.sum(p * dp, axis=1, keepdims=True) for p, dp in found]
                )
                for (t, lo, hi), (p, dp) in zip(block_pieces(b), found):
                    score_tiles[t].append(spread((p * (dp - shared)).astype(BF16), t, lo, hi))
            res = [None] * blocks
            for t in range(tiles):
                first, last = tile_rows(t)
                part = mm(jnp.concatenate(score_tiles[t], axis=0), kg[t * GROUP : (t + 1) * GROUP])
                for i in range((last - first) // BLOCK):
                    b = first // BLOCK + i
                    piece = part[i * BLOCK : (i + 1) * BLOCK]
                    res[b] = piece if res[b] is None else res[b] + piece
            out = jnp.where(in_head[h], jnp.concatenate(res, axis=0), out)
        query_part = mm(red[...], out.astype(BF16), TN)[0:8] * (2.0 * HEAD_DIM**-0.5)
        acc_ref[0:8, lanes] = acc_in_ref[0:8, lanes] + query_part
        cross = mm(pr[:, lanes], gg, TN)
        value_part = jnp.zeros((8, GROUP), F32)
        for h in range(per_group):
            top = ((h + 1) % per_group) * HEAD_DIM + 8
            value_part = jnp.where(in_head[h], cross[top : top + 8], value_part)
        acc_ref[8:16, lanes] = acc_in_ref[8:16, lanes] + 2.0 * value_part
        return carry

    lax.fori_loop(0, groups, attention_back, 0)

    acc_ref[16:17, :] = acc_in_ref[16:17, :] + head_grad
    lane_row = lax.broadcasted_iota(jnp.int32, (1, width), 1)
    extras = jnp.where(
        lane_row == 0,
        loss,
        jnp.where(lane_row == 1, items, jnp.where(lane_row == 2, weight_sum, 0.0)),
    )
    acc_ref[17:18, :] = acc_in_ref[17:18, :] + extras
    acc_ref[18:24, :] = jnp.zeros((6, width), F32)


def layer_call(x, seg, label, small, weights, acc_in):
    pos, gain, shift, bias, down, up, head, ffb = small
    wqkv, wo, win, wout = weights
    parts, rows, _ = x.shape
    width = pos.shape[1]
    hidden = wout.shape[0]
    heads = width // HEAD_DIM
    tiles = rows // GROUP
    vmem = pl.BlockSpec(memory_space=pltpu.VMEM)
    hbm = pl.BlockSpec(memory_space=pl.ANY)
    scratch = [
        pltpu.VMEM(wqkv.shape, BF16),
        pltpu.VMEM(wo.shape, BF16),
        pltpu.VMEM(win.shape, BF16),
        pltpu.VMEM(wout.shape, BF16),
        pltpu.VMEM((rows, width), BF16),
        pltpu.VMEM((rows, width), F32),
        pltpu.VMEM((rows, width), BF16),
        pltpu.VMEM((rows, width), BF16),
        pltpu.VMEM((rows, width), BF16),
        pltpu.VMEM((rows, GROUP), BF16),
        pltpu.VMEM((8, 128), BF16),
        pltpu.VMEM((rows, width), BF16),
        pltpu.VMEM((heads, tiles, 3 * BLOCK, GROUP), BF16),
        pltpu.VMEM((rows, width), BF16),
        pltpu.VMEM((rows, width), F32),
        pltpu.VMEM((rows, 1), F32),
        pltpu.VMEM((rows, width), F32),
        pltpu.VMEM((rows, hidden), F32),
        pltpu.VMEM((rows, hidden), BF16),
        pltpu.SemaphoreType.DMA((4,)),
    ]
    flops = 2 * rows * (width * width * 5 + 4 * width * hidden + 4 * rows * width)
    return pl.pallas_call(
        layer_kernel,
        out_shape=jax.ShapeDtypeStruct(acc_in.shape, F32),
        in_specs=[vmem] * 12 + [hbm] * 4,
        out_specs=vmem,
        scratch_shapes=scratch,
        compiler_params=pltpu.CompilerParams(vmem_limit_bytes=58 * 1024 * 1024),
        cost_estimate=pl.CostEstimate(
            flops=flops, bytes_accessed=16 * 1024 * 1024, transcendentals=3 * rows * hidden
        ),
        name="layer",
    )(x, seg, label, pos, gain, shift, bias, down, up, head, ffb, acc_in, wqkv, wo, win, wout)


def newton_schulz_orthogonal(moment):
    basis = moment / (jnp.sqrt(jnp.sum(moment * moment)) + 1e-07)
    for sweep in range(5):
        gram = jnp.dot(basis, basis.T, precision=TOP_PRECISION)
        poly = NS_B * gram + NS_C * jnp.dot(gram, gram, precision=TOP_PRECISION)
        basis = NS_A * basis + jnp.dot(poly, basis, precision=TOP_PRECISION)
    return basis


def local(
    input_token_ids,
    segments,
    labels,
    embedding,
    position_embedding_table,
    norm_gain_rows,
    norm_shift_rows,
    query_key_value_weight,
    attention_output_weight,
    attention_bias_stack,
    feedforward_in_weight,
    feedforward_bias,
    feedforward_out_weight,
    adapter_down_weight,
    adapter_up_weight,
    adapter_momentum,
    head,
    head_first_moment,
    head_second_moment,
):
    length = input_token_ids.shape[-1]
    slots = labels.shape[-1]
    width = position_embedding_table.shape[1]
    rank = adapter_up_weight.shape[1]
    ids = input_token_ids.reshape(-1, length)
    segs = segments.reshape(-1, 1, length)
    labs = labels.reshape(-1, 1, slots)
    units = ids.shape[0]
    feats = embedding.shape[0]

    win = lax.all_gather(feedforward_in_weight, "tensor", axis=0)
    wout = lax.all_gather(feedforward_out_weight, "tensor", axis=0, tiled=True)
    ffb = lax.all_gather(feedforward_bias, "tensor", axis=0, tiled=True).astype(F32)[None, :]

    all_ids = lax.all_gather(ids, "tensor", axis=0)
    parts = all_ids.shape[0]
    picked = jnp.take(embedding, all_ids.reshape(-1), axis=1).T.reshape(parts, units, length, feats)

    down = jnp.concatenate(
        [adapter_down_weight[0], adapter_down_weight[1], jnp.zeros((width, HEAD_DIM - 2 * rank), BF16)], axis=1
    )
    down = jnp.concatenate([down] * (GROUP // HEAD_DIM), axis=1)
    twice = 2.0 * adapter_up_weight.astype(BF16)
    up = jnp.stack(
        [
            jnp.pad(twice[0], ((0, GROUP - rank), (0, 0))),
            jnp.pad(twice[1], ((rank, GROUP - 2 * rank), (0, 0))),
        ]
    )
    small = (
        position_embedding_table,
        norm_gain_rows,
        norm_shift_rows,
        attention_bias_stack,
        down,
        up,
        head[None, :],
        ffb,
    )
    weights = (query_key_value_weight, attention_output_weight, win, wout)
    acc = jnp.zeros((24, width), F32)
    for u in range(units):
        x = lax.all_to_all(picked[:, u], "tensor", split_axis=0, concat_axis=0, tiled=True)
        acc = layer_call(x, segs[u], labs[u], small, weights, acc)
    acc = lax.psum(acc, ("dp", "tensor"))

    loss_total = acc[17, 0]
    item_total = acc[17, 1]
    adapter_gradient_sum = acc[0:16].reshape(2, rank, width) / item_total
    head_gradient_sum = jnp.concatenate([acc[16], acc[17, 2:3]]) / item_total
    global_gradient_norm = jnp.sqrt(
        jnp.sum(adapter_gradient_sum * adapter_gradient_sum)
        + jnp.sum(head_gradient_sum * head_gradient_sum)
    )
    scale_factor = jnp.minimum(1.0, CLIP_NORM / (global_gradient_norm + 1e-06))
    adapter_moment_next = ORTHO_MOMENTUM * adapter_momentum + scale_factor * adapter_gradient_sum
    orthogonal_update = jnp.stack(
        [
            newton_schulz_orthogonal(adapter_moment_next[0]),
            newton_schulz_orthogonal(adapter_moment_next[1]),
        ]
    )
    adapter_up_updated = adapter_up_weight - ORTHO_STEP_SIZE * orthogonal_update
    clipped = scale_factor * head_gradient_sum
    head_moment_next = BETA_ONE * head_first_moment + (1.0 - BETA_ONE) * clipped
    head_square_next = BETA_TWO * head_second_moment + (1.0 - BETA_TWO) * clipped * clipped
    first_hat = head_moment_next / (1.0 - BETA_ONE**STEP)
    second_hat = head_square_next / (1.0 - BETA_TWO**STEP)
    head_updated = head - ADAM_RATE * (first_hat / (jnp.sqrt(second_hat) + ADAM_EPS) + DECAY * head)
    return (
        loss_total,
        item_total,
        global_gradient_norm,
        adapter_moment_next,
        adapter_up_updated,
        adapter_up_updated.astype(jnp.bfloat16),
        head_moment_next,
        head_square_next,
        head_updated,
        head_updated.astype(jnp.bfloat16),
    )


def solution(mesh):
    placed = (
        P(None, ("dp", "tensor"), None),
        P(None, ("dp", "tensor"), None),
        P(None, ("dp", "tensor"), None),
        P("tensor", None),
        P(),
        P(),
        P(),
        P(),
        P(),
        P(),
        P(None, "tensor"),
        P("tensor"),
        P("tensor", None),
        P(),
        P(),
        P(),
        P(),
        P(),
        P(),
    )
    return jax.shard_map(
        local,
        mesh=mesh,
        in_specs=placed,
        out_specs=(P(), P(), P(), P(), P(), P(), P(), P(), P(), P()),
        check_vma=False,
    )
```

time: 1480 us -> 475 us (0.32)
  matrix products: 419 us -> 4.72 us
  waiting for transfers between devices: 480 us -> 152 us
  local copies, waits for them, and re-layouts: 275 us -> 92.3 us
  Pallas kernels: 0 us -> 150 us
  other arithmetic: 139 us -> 16.3 us
  blocking collectives: 109 us -> 17.7 us
    dot_general x64 -> x0, matrix products: 366 us -> none  [the longest x4 75.3 us: ffn_forward(): jnp.dot(lax.all_gather(normed1_r, 'tensor', axis=0, tiled=True), input_we...]
    reduce_scatter x8 -> x0, waiting for transfers between devices: 311 us -> none  [the longest x4 158 us: ffn_backward(): lax.psum_scatter(lax.dot_general(grad_pre, input_weight, CONTRACT, prefer...]
    all_gather x8 -> x2, waiting for transfers between devices: 161 us -> 0.01 us  [the longest x1 0.01 us: local(): win = lax.all_gather(feedforward_in_weight, 'tensor', axis=0)]
    pallas_call x0 -> x4, Pallas kernels: none -> 150 us  [layer_call(): pl.pallas_call(layer_kernel, out_shape=jax.ShapeDtypeStruct(acc_in.shape,...]
    psum x0 -> x1, waiting for transfers between devices: none -> 119 us  [local(): acc = lax.psum(acc, ('dp', 'tensor'))]
    psum x2 -> x0, blocking collectives: 79.7 us -> none  [the longest x1 40.3 us: local(): lax.psum((adapter_loss_piece, head_loss_piece, loss_piece), ('dp', 'tenso...]
    gather x8 -> x1, local copies, waits for them, and re-layouts: 100 us -> 42.6 us  [local(): jnp.take(embedding, all_ids.reshape(-1), axis=1)]
    reduce_sum x30 -> x0, other arithmetic: 46 us -> none  [the longest x5 14.7 us: layer_norm(): center = jnp.mean(value_rows, -1, keepdims=True)]
  transfers between devices with their start and end apart: 20 -> 7, of which waited for: 17 -> 4; matrix products, arithmetic and copies ran while one was open for 26% -> 21% of each run, Pallas kernels for 0% -> 0%
where the time goes in v1:
time: 475 us; the launch traced here: 467 us
  waiting for transfers between devices  152 us (32%)
  Pallas kernels  150 us (32%)
  local copies, waits for them, and re-layouts  92.3 us (19%)
  between operations  18.3 us (4%)
  blocking collectives  17.7 us (4%)
  other arithmetic  16.3 us (3%)
  starting transfers between devices  15.7 us (3%)
    pallas_call x4, Pallas kernels, layer_call(): pl.pallas_call(layer_kernel, out_shape=jax.ShapeDtypeStruct(acc_in.shape,...  150 us
    psum x1, waiting for transfers between devices, local(): acc = lax.psum(acc, ('dp', 'tensor'))  119 us
    gather x1, local copies, waits for them, and re-layouts, local(): jnp.take(embedding, all_ids.reshape(-1), axis=1)  42.6 us
    all_to_all x4, waiting for transfers between devices, local(): lax.all_to_all(picked[:, u], 'tensor', split_axis=0, concat_axis=0, tiled...  31.3 us
    unnamed x26, local copies, waits for them, and re-layouts  28.8 us
    all_to_all x4, starting transfers between devices, local(): lax.all_to_all(picked[:, u], 'tensor', split_axis=0, concat_axis=0, tiled...  15.5 us
    all_gather x1, blocking collectives, local(): lax.all_gather(feedforward_bias, 'tensor', axis=0, tiled=True).astype(F32)  11.6 us
  transfers between devices with their start and end apart: 7, of which 4 were waited for; matrix products, arithmetic and copies ran while one was open for 21% of the time, Pallas kernels for 0%

profile of v1, /device:TPU:0, one launch (start us, length us, event | category | flops | bytes accessed | tf_op | source)
XLA Modules:
  0.0 466.6 jit_solution(348362435175422130)
XLA Ops:
  8.7 28.4 %copy.52 = bf16[192,50265]{0,1:T(8,128)(2,1)} copy(bf16[192,50265]{1,0:T(8,128)(2,1)} %param.22) | data formatting | bytes 38603520 | tf_op args[3]
  37.1 6.2 %all-gather = s32[16,1,512]{2,1,0:T(1,128)S(1)} all-gather(s32[4,1,512]{2,1,0:T(1,128)S(1)} %copy-done.5), channel_id=2, replica_groups=mesh['dp'=8,'tensor'=4] {'tensor'}, dimensions={0}, use_global_device_ids=true | all-gather | bytes 40960 | tf_op jit(solution)/shard_map/all_gather | solution.py:474
  43.3 42.6 %gather_fusion = bf16[8192,192]{1,0:T(8,128)(2,1)} fusion(bf16[192,50265]{0,1:T(8,128)(2,1)} %copy.52, s32[8192]{0:T(1024)S(1)} %broadcast_clamp_fusion), kind=kCustom, calls=%fused_computation | custom fusion | bytes 6324224 | tf_op jit(solution)/shard_map/jit(_take)/gather | solution.py:476
  85.9 6.0 %broadcast_select_fusion = bf16[8192,192]{1,0:T(8,128)(2,1)S(1)} fusion(bf16[8192,192]{1,0:T(8,128)(2,1)} %gather_fusion, pred[8192]{0:T(1024)(128)(4,1)S(1)} %compare_and_fusion), kind=kLoop, calls=%fused_computation.1 | loop fusion | flops 1572864 | bytes 6299648 | tf_op jit(solution)/shard_map/jit(_take)/select_n | solution.py:476
  91.9 1.3 fusion.22
  93.2 2.2 copy.54
  95.4 4.2 all-to-all-start
  99.6 1.2 copy.57
  100.9 10.6 %all-to-all-done = bf16[4,512,192]{1,2,0:T(8,128)(2,1)} async-done(((bf16[4,512,192]{1,2,0:T(8,128)(2,1)}), bf16[4,512,192]{1,2,0:T(8,128)(2,1)}, u32[]{:S(2)}, u32[]{:S(2)}) %all-to-all-start) | async-done | bytes 786464 | tf_op jit(solution)/shard_map/all_to_all | solution.py:502
  111.4 3.5 all-to-all-start.1
  115.0 1.2 copy.58
  116.2 1.2 copy.59
  117.4 9.1 %all-to-all-done.1 = bf16[4,512,192]{1,2,0:T(8,128)(2,1)S(1)} async-done(((bf16[4,512,192]{1,2,0:T(8,128)(2,1)}), bf16[4,512,192]{1,2,0:T(8,128)(2,1)S(1)}, u32[]{:S(2)}, u32[]{:S(2)}) %all-to-all-start.1) | async-done | bytes 786464 | tf_op jit(solution)/shard_map/all_to_all | solution.py:502
  126.6 3.6 all-to-all-start.2
  130.3 11.6 %all-to-all-done.2 = bf16[4,512,192]{1,2,0:T(8,128)(2,1)S(1)} async-done(((bf16[4,512,192]{1,2,0:T(8,128)(2,1)}), bf16[4,512,192]{1,2,0:T(8,128)(2,1)S(1)}, u32[]{:S(2)}, u32[]{:S(2)}) %all-to-all-start.2) | async-done | bytes 786464 | tf_op jit(solution)/shard_map/all_to_all | solution.py:502
  141.8 4.2 all-to-all-start.3
  147.1 11.6 %all-gather.2 = bf16[4,1,768]{2,1,0:T(2,128)(2,1)S(1)} all-gather(bf16[1,1,768]{2,1,0:T(2,128)(2,1)S(1)} %reshape.93), channel_id=1, replica_groups=mesh['dp'=8,'tensor'=4] {'tensor'}, dimensions={0}, use_global_device_ids=true | all-gather | bytes 7680 | tf_op jit(solution)/shard_map/all_gather | solution.py:472
  159.3 2.0 concatenate.8.down_ref
  163.4 2.2 copy.63.x_ref
  165.6 1.3 copy.62.x_ref
  166.9 1.3 copy.61.x_ref
  168.2 2.2 copy.60.x_ref
  171.0 37.5 %layer.4.acc_in_ref = f32[24,768]{1,0:T(8,128)} custom-call(bf16[4,512,192]{2,1,0:T(8,128)(2,1)} %copy.60.x_ref, s32[1,512]{1,0:T(1,128)} %get-tuple-element.29.seg_ref, f32[1,64]{1,0:T(1,128)} %get-tuple-element.33.label_ref, bf16[512,768]{1,0:T(8,128)(2,1)} %pos_ref.7, f32[3,768]{1,0:T(4,128)} %gain_ref.7, f32[3,768]{1,0:T(4,128)} %shift_ref.7, ...), custom_call_target="tpu_custom_call" | custom-call | flops 14294188032 | bytes 16777216 | tf_op jit(solution)/shard_map/layer/pallas_call | solution.py:416
  208.6 37.3 %layer.5.acc_in_ref = f32[24,768]{1,0:T(8,128)} custom-call(bf16[4,512,192]{2,1,0:T(8,128)(2,1)} %copy.61.x_ref, s32[1,512]{1,0:T(1,128)} %get-tuple-element.32.seg_ref, f32[1,64]{1,0:T(1,128)} %get-tuple-element.36.label_ref, bf16[512,768]{1,0:T(8,128)(2,1)} %pos_ref.7, f32[3,768]{1,0:T(4,128)} %gain_ref.7, f32[3,768]{1,0:T(4,128)} %shift_ref.7, ...), custom_call_target="tpu_custom_call" | custom-call | flops 14294188032 | bytes 16777216 | tf_op jit(solution)/shard_map/layer/pallas_call | solution.py:416
  245.9 37.5 %layer.6.acc_in_ref = f32[24,768]{1,0:T(8,128)} custom-call(bf16[4,512,192]{2,1,0:T(8,128)(2,1)} %copy.62.x_ref, s32[1,512]{1,0:T(1,128)} %get-tuple-element.30.seg_ref, f32[1,64]{1,0:T(1,128)} %get-tuple-element.34.label_ref, bf16[512,768]{1,0:T(8,128)(2,1)} %pos_ref.7, f32[3,768]{1,0:T(4,128)} %gain_ref.7, f32[3,768]{1,0:T(4,128)} %shift_ref.7, ...), custom_call_target="tpu_custom_call" | custom-call | flops 14294188032 | bytes 16777216 | tf_op jit(solution)/shard_map/layer/pallas_call | solution.py:416
  283.4 37.4 %layer.7 = f32[24,768]{1,0:T(8,128)} custom-call(bf16[4,512,192]{2,1,0:T(8,128)(2,1)} %copy.63.x_ref, s32[1,512]{1,0:T(1,128)} %get-tuple-element.31.seg_ref, f32[1,64]{1,0:T(1,128)} %get-tuple-element.35.label_ref, bf16[512,768]{1,0:T(8,128)(2,1)} %pos_ref.7, f32[3,768]{1,0:T(4,128)} %gain_ref.7, f32[3,768]{1,0:T(4,128)} %shift_ref.7, f32[5,768]{1,0:T(8,128)} %bias_ref.7, ...), custom_call_target="tpu_custom_call" | custom-call | flops 14294188032 | bytes 16777216 | tf_op jit(solution)/shard_map/layer/pallas_call | solution.py:416
  320.9 119.3 %all-reduce.4.cloned.1.call-done = f32[24,768]{1,0:T(8,128)} async-done(((f32[24,768]{1,0:T(8,128)}), f32[24,768]{1,0:T(8,128)}) %all-reduce.4.cloned.1.call-update) | async-done | bytes 73744 | tf_op jit(solution)/shard_map/psum | solution.py:504
  440.2 1.5 fusion.23
  442.4 1.9 multiply_reduce_fusion.3
  444.3 2.1 multiply_reduce_fusion
  447.8 1.5 bitcast_add_fusion
  456.7 2.0 fusion.19
  (81 shorter events, 12.7 us)
Async XLA Ops:
  7.2 163.2 %all-gather.8.cloned.1.call-start = ((), (), s32[]{:S(2)}) async-start(), calls=%async_computation.6 | async-start | bytes 5898240 | tf_op jit(solution)/shard_map/all_gather | solution.py:470
  7.9 162.5 %all-gather.6.cloned.1.call-start = ((), (), s32[]{:S(2)}) async-start(), calls=%async_computation.4 | async-start | bytes 5898240 | tf_op jit(solution)/shard_map/all_gather | solution.py:471
  8.7 28.4 %copy-start.5 = (s32[4,1,512]{2,1,0:T(1,128)S(1)}, s32[4,1,512]{2,1,0:T(1,128)}, u32[]{:S(2)}) copy-start(s32[4,1,512]{2,1,0:T(1,128)} %param.19) | copy-start | bytes 24580
  95.4 16.1 %all-to-all-start = ((bf16[4,512,192]{1,2,0:T(8,128)(2,1)}), bf16[4,512,192]{1,2,0:T(8,128)(2,1)}, u32[]{:S(2)}, u32[]{:S(2)}) async-start(bf16[4,512,192]{1,2,0:T(8,128)(2,1)} %bitcast.127), calls=%async_computation | async-start | bytes 1572864 | tf_op jit(solution)/shard_map/all_to_all | solution.py:502
  99.6 30.6 %copy-start.3 = (bf16[2,768,8]{1,2,0:T(8,128)(2,1)S(1)}, bf16[2,768,8]{1,2,0:T(8,128)(2,1)}, u32[]{:S(2)}) copy-start(bf16[2,768,8]{1,2,0:T(8,128)(2,1)} %param.32) | copy-start | bytes 73732
  99.6 30.6 %copy-start = (f32[2,8,768]{2,1,0:T(8,128)S(1)}, f32[2,8,768]{2,1,0:T(8,128)}, u32[]{:S(2)}) copy-start(f32[2,8,768]{2,1,0:T(8,128)} %param.33) | copy-start | bytes 147460
  111.4 15.1 %all-to-all-start.1 = ((bf16[4,512,192]{1,2,0:T(8,128)(2,1)}), bf16[4,512,192]{1,2,0:T(8,128)(2,1)S(1)}, u32[]{:S(2)}, u32[]{:S(2)}) async-start(bf16[4,512,192]{1,2,0:T(8,128)(2,1)} %bitcast.126), calls=%async_computation.1 | async-start | bytes 1572864 | tf_op jit(solution)/shard_map/all_to_all | solution.py:502
  114.9 31.5 %copy-start.4 = (f32[769]{0:T(1024)S(1)}, f32[769]{0:T(1024)}, u32[]{:S(2)}) copy-start(f32[769]{0:T(1024)} %param.35) | copy-start | bytes 9232
  115.0 32.1 %copy-start.9 = (bf16[768]{0:T(1024)(128)(2,1)S(1)}, bf16[768]{0:T(1024)(128)(2,1)}, u32[]{:S(2)}) copy-start(bf16[768]{0:T(1024)(128)(2,1)} %param.30) | copy-start | bytes 4612
  126.6 35.7 %copy-start.10 = (f32[4,1,64]{2,1,0:T(1,128)S(1)}, f32[4,1,64]{2,1,0:T(1,128)}, u32[]{:S(2)}) copy-start(f32[4,1,64]{2,1,0:T(1,128)} %param.21) | copy-start | bytes 3076
  126.6 36.2 %copy-start.6 = (s32[4,1,512]{2,1,0:T(1,128)S(1)}, s32[4,1,512]{2,1,0:T(1,128)}, u32[]{:S(2)}) copy-start(s32[4,1,512]{2,1,0:T(1,128)} %param.20) | copy-start | bytes 24580
  126.6 15.3 %all-to-all-start.2 = ((bf16[4,512,192]{1,2,0:T(8,128)(2,1)}), bf16[4,512,192]{1,2,0:T(8,128)(2,1)S(1)}, u32[]{:S(2)}, u32[]{:S(2)}) async-start(bf16[4,512,192]{1,2,0:T(8,128)(2,1)} %bitcast.125), calls=%async_computation.2 | async-start | bytes 1572864 | tf_op jit(solution)/shard_map/all_to_all | solution.py:502
  141.8 26.4 %all-to-all-start.3 = ((bf16[4,512,192]{1,2,0:T(8,128)(2,1)}), bf16[4,512,192]{1,2,0:T(8,128)(2,1)}, u32[]{:S(2)}, u32[]{:S(2)}) async-start(bf16[4,512,192]{1,2,0:T(8,128)(2,1)} %bitcast.21), calls=%async_computation.3 | async-start | bytes 1572864 | tf_op jit(solution)/shard_map/all_to_all | solution.py:502
  146.0 294.1 %all-reduce.4.cloned.1.call-start = ((), (), s32[]{:S(2)}) async-start(), calls=%async_computation.5 | async-start | bytes 147456 | tf_op jit(solution)/shard_map/psum | solution.py:504
  283.4 164.4 %copy-start.2 = (f32[2,8,768]{2,1,0:T(8,128)S(1)}, f32[2,8,768]{2,1,0:T(8,128)}, u32[]{:S(2)}) copy-start(f32[2,8,768]{2,1,0:T(8,128)} %param.34) | copy-start | bytes 147460
  283.4 173.3 %copy-start.7 = (f32[769]{0:T(1024)S(1)}, f32[769]{0:T(1024)}, u32[]{:S(2)}) copy-start(f32[769]{0:T(1024)} %param.37) | copy-start | bytes 9232
  283.4 173.3 %copy-start.8 = (f32[769]{0:T(1024)S(1)}, f32[769]{0:T(1024)}, u32[]{:S(2)}) copy-start(f32[769]{0:T(1024)} %param.36) | copy-start | bytes 9232
  449.2 9.4 %copy-start.1 = (f32[2,8,768]{2,1,0:T(8,128)}, f32[2,8,768]{2,1,0:T(8,128)S(1)}, u32[]{:S(2)}) copy-start(f32[2,8,768]{2,1,0:T(8,128)S(1)} %bitcast_add_fusion) | copy-start | bytes 147460
Sparse Core Ops, SparseCore 0:
  9.6 40.3 all-gather.7
  51.5 37.4 all-gather.5
  321.0 119.1 all-reduce.3
